TPU v7x, 32 devices: a whole 2x2x4 slice. The times are simulated.
32 devices in a mesh: dp: 16 (over z, y, x), seq: 2 (over core).
Axes of the slice: x: 2, y: 2, z: 4, core: 2. Of those that a mesh axis runs over, the one named last changes fastest.
Arguments:
- tokens: bfloat16 [32, 256, 1024], P('dp', 'seq'), may hold values from -6 to 6
- condition: bfloat16 [32, 768], P('dp'), may hold values from -6 to 6
- positions: int32 [32, 2, 256], P('dp', None, 'seq'), may hold values from 0 to 15, as said below
- weight_codes: int32 [32], P('dp'), may hold values from 0 to 31
- loss_table: float32 [32], replicated, may hold values from 0.25 to 4
- out_grad: bfloat16 [32, 256, 1024], P('dp', 'seq'), may hold values from -6 to 6
- mod_attn: bfloat16 [768, 1024], P('seq'), may hold values from -0.109375 to 0.109375
- qkv_weight: bfloat16 [1024, 3072], P('seq'), may hold values from -0.1875 to 0.1875
- attn_scale: float32 [16], replicated, may hold values from 8 to 24
- out_weight: bfloat16 [1024, 1024], P('seq'), may hold values from -1.5 to 1.5
- mod_ff: bfloat16 [768, 1024], P('seq'), may hold values from -0.109375 to 0.109375
- up_weight: bfloat16 [1024, 6144], P('seq'), may hold values from -0.1875 to 0.1875
- down_weight: bfloat16 [3072, 1024], P('seq'), may hold values from -0.109375 to 0.109375
Outputs:
- mixed: bfloat16 [32, 256, 1024], P('dp', 'seq')
- tokens_grad: float32 [32, 256, 1024], P('dp', 'seq')
- condition_grad: float32 [32, 768], P('dp')
- mod_attn_grad: float32 [768, 1024], P('seq', 'dp')
- qkv_grad: float32 [1024, 3072], P('seq', 'dp')
- scale_grad: float32 [16], replicated
- out_weight_grad: float32 [1024, 1024], P('seq', 'dp')
- mod_ff_grad: float32 [768, 1024], P('seq', 'dp')
- up_grad: float32 [1024, 6144], P('seq', 'dp')
- down_grad: float32 [3072, 1024], P('seq', 'dp')
Inputs may be any that keep to these rules, and one draw needn't show every extreme that they name: `positions`: for each image the 256 pairs (row, column) along the middle dimension are the cells of a 16 x 16 grid, each exactly once.
All inputs are finite; a program needn't handle non-finite values.
Results may differ from a plain program's by a relative error of at most 0.023.
Values may be sent and summed in bfloat16 or wider, within the bound.
No kernel may reach another device: no remote copies, remote signals or barrier semaphores. Data moves between devices by JAX's collectives and lax.ppermute only.
A program may use at most 256 MiB of HBM per device.

v0:
```python
import math

import jax
import jax.numpy as jnp
from jax import lax
from jax.sharding import PartitionSpec as P

HEADS = 16
HEAD_DIM = 64
GRID = 16


epsilon = 1e-06
finest = lax.Precision.HIGHEST


def norm_mod(values, modulation):
    return (
        values
        * lax.rsqrt(jnp.mean(values * values, axis=-1, keepdims=True) + epsilon)
        * (1.0 + modulation[:, None, :])
    )


def angle_tables(positions):
    quarter = HEAD_DIM // 8
    counter = jnp.arange(quarter)[None, :] * HEADS + jnp.arange(HEADS)[:, None]
    frequency = math.pi * jnp.power(10.0, counter.astype(jnp.float32) / (HEADS * quarter))
    coords = (2.0 * positions.astype(jnp.float32) + 1.0) / GRID - 1.0
    angles = jnp.concatenate(
        [coords[:, 0, :, None, None] * frequency, coords[:, 1, :, None, None] * frequency], axis=-1
    )
    return (jnp.cos(angles), jnp.sin(angles))


def rotate(vectors, cosine_table, sine_table):
    rot_width = cosine_table.shape[-1]
    first = vectors[..., :rot_width]
    second = vectors[..., rot_width : 2 * rot_width]
    return jnp.concatenate(
        [
            first * cosine_table - second * sine_table,
            second * cosine_table + first * sine_table,
            vectors[..., 2 * rot_width :],
        ],
        axis=-1,
    )


def query_key(queries, keys_raw, attn_scale, cosine_table, sine_table):
    root_scale = jnp.sqrt(attn_scale)[:, None]
    queries = (
        queries
        * lax.rsqrt(jnp.sum(queries * queries, axis=-1, keepdims=True) + epsilon)
        * root_scale
    )
    keys_raw = (
        keys_raw
        * lax.rsqrt(jnp.sum(keys_raw * keys_raw, axis=-1, keepdims=True) + epsilon)
        * root_scale
    )
    return (rotate(queries, cosine_table, sine_table), rotate(keys_raw, cosine_table, sine_table))


def gated_gelu(projected):
    middle = projected.shape[-1] // 2
    return projected[..., :middle] * jax.nn.gelu(projected[..., middle:], approximate=False)


def shards(
    tokens,
    condition,
    positions,
    weight_codes,
    loss_table,
    out_grad,
    mod_attn,
    qkv_weight,
    attn_scale,
    out_weight,
    mod_ff,
    up_weight,
    down_weight,
):
    gathered = (
        lax.all_gather(mod_attn, "seq", axis=0, tiled=True),
        lax.all_gather(qkv_weight, "seq", axis=0, tiled=True),
        lax.all_gather(out_weight, "seq", axis=0, tiled=True),
        lax.all_gather(mod_ff, "seq", axis=0, tiled=True),
        lax.all_gather(up_weight, "seq", axis=0, tiled=True),
        lax.all_gather(down_weight, "seq", axis=0, tiled=True),
    )
    attn_mod_full, qkv_full, out_full, ff_mod_full, up_full, down_full = gathered
    images, length, model_width = tokens.shape
    head_count = attn_scale.shape[0]
    head_shape = (images, length, head_count, model_width // head_count)
    mod_one = jnp.dot(condition, attn_mod_full, preferred_element_type=jnp.float32)
    mod_two = jnp.dot(condition, ff_mod_full, preferred_element_type=jnp.float32)
    inputs = tokens.astype(jnp.float32)
    hidden_one = norm_mod(inputs, mod_one).astype(jnp.bfloat16)
    projected = jnp.einsum("ild,de->ile", hidden_one, qkv_full, preferred_element_type=jnp.float32)
    q_raw = projected[..., :model_width].reshape(head_shape)
    k_raw = projected[..., model_width : 2 * model_width].reshape(head_shape)
    cosine_table, sine_table = angle_tables(positions)
    query_rot, key_rot = query_key(q_raw, k_raw, attn_scale, cosine_table, sine_table)
    query_low = query_rot.astype(jnp.bfloat16)
    key_low = key_rot.reshape(images, length, model_width).astype(jnp.bfloat16)
    value_low = projected[..., 2 * model_width :].astype(jnp.bfloat16)
    key_all, value_all = (
        lax.all_gather(key_low, "seq", axis=1, tiled=True),
        lax.all_gather(value_low, "seq", axis=1, tiled=True),
    )
    total_len = key_all.shape[1]
    all_shape = (images, total_len, head_count, model_width // head_count)
    key_heads = key_all.reshape(all_shape)
    value_heads = value_all.reshape(all_shape)
    scores = jnp.einsum("ilhc,ishc->ihls", query_low, key_heads, preferred_element_type=jnp.float32)
    row_peak = jnp.max(scores, axis=-1, keepdims=True)
    exponent = jnp.exp(scores - row_peak)
    row_total = jnp.sum(exponent, axis=-1, keepdims=True)
    prob_low = (exponent / row_total).astype(jnp.bfloat16)
    log_total = row_peak + jnp.log(row_total)
    attended = jnp.einsum(
        "ihls,ishc->ilhc", prob_low, value_heads, preferred_element_type=jnp.float32
    )
    attended = attended.reshape(images, length, model_width).astype(jnp.bfloat16)
    residual = inputs + jnp.einsum(
        "ild,de->ile", attended, out_full, preferred_element_type=jnp.float32
    )
    hidden_two = norm_mod(residual, mod_two).astype(jnp.bfloat16)
    gate_up = jnp.einsum("ild,de->ile", hidden_two, up_full, preferred_element_type=jnp.float32)
    activated = gated_gelu(gate_up).astype(jnp.bfloat16)
    mixed = (
        residual
        + jnp.einsum("ilf,fd->ild", activated, down_full, preferred_element_type=jnp.float32)
    ).astype(jnp.bfloat16)
    back_set = (
        lax.all_gather(mod_attn, "seq", axis=0, tiled=True),
        lax.all_gather(qkv_weight, "seq", axis=0, tiled=True),
        lax.all_gather(out_weight, "seq", axis=0, tiled=True),
        lax.all_gather(mod_ff, "seq", axis=0, tiled=True),
        lax.all_gather(up_weight, "seq", axis=0, tiled=True),
        lax.all_gather(down_weight, "seq", axis=0, tiled=True),
    )
    attn_mod_full, qkv_full, out_full, ff_mod_full, up_full, down_full = back_set
    levels = loss_table.shape[0]
    picked = (weight_codes[:, None] == jnp.arange(levels)[None, :]).astype(jnp.float32)
    image_scale = jnp.sum(picked * loss_table[None, :], axis=1)
    cotangent = out_grad.astype(jnp.float32) * image_scale[:, None, None]
    cot_low = cotangent.astype(jnp.bfloat16)
    down_term = jnp.einsum("ilf,ild->fd", activated, cot_low, preferred_element_type=jnp.float32)
    active_grad = jnp.einsum("ild,fd->ilf", cot_low, down_full, preferred_element_type=jnp.float32)
    gate_up_grad = jax.vjp(gated_gelu, gate_up)[1](active_grad)[0].astype(jnp.bfloat16)
    up_term = jnp.einsum(
        "ild,ile->de", hidden_two, gate_up_grad, preferred_element_type=jnp.float32
    )
    hidden_two_grad = jnp.einsum(
        "ile,de->ild", gate_up_grad, up_full, preferred_element_type=jnp.float32
    )
    _, second_pull = jax.vjp(norm_mod, residual, mod_two)
    residual_part, mod_two_grad = second_pull(hidden_two_grad)
    residual_grad = cotangent + residual_part
    residual_low = residual_grad.astype(jnp.bfloat16)
    out_term = jnp.einsum("ild,ile->de", attended, residual_low, preferred_element_type=jnp.float32)
    attended_grad = jnp.einsum(
        "ile,de->ild", residual_low, out_full, preferred_element_type=jnp.float32
    ).astype(jnp.bfloat16)
    grad_heads = attended_grad.reshape(head_shape)
    scores = jnp.einsum("ilhc,ishc->ihls", query_low, key_heads, preferred_element_type=jnp.float32)
    prob_again = jnp.exp(scores - log_total)
    prob_again_low = prob_again.astype(jnp.bfloat16)
    prob_grad = jnp.einsum(
        "ilhc,ishc->ihls", grad_heads, value_heads, preferred_element_type=jnp.float32
    )
    score_grad = (
        prob_again * (prob_grad - jnp.sum(prob_again * prob_grad, axis=-1, keepdims=True))
    ).astype(jnp.bfloat16)
    query_grad = jnp.einsum(
        "ihls,ishc->ilhc", score_grad, key_heads, preferred_element_type=jnp.float32
    )
    key_terms = jnp.einsum(
        "ihls,ilhc->ishc", score_grad, query_low, preferred_element_type=jnp.float32
    ).reshape(images, total_len, model_width)
    value_terms = jnp.einsum(
        "ihls,ilhc->ishc", prob_again_low, grad_heads, preferred_element_type=jnp.float32
    ).reshape(images, total_len, model_width)
    key_grad, value_grad = (
        lax.psum_scatter(
            key_terms.astype(jnp.bfloat16), "seq", scatter_dimension=1, tiled=True
        ).astype(jnp.float32),
        lax.psum_scatter(
            value_terms.astype(jnp.bfloat16), "seq", scatter_dimension=1, tiled=True
        ).astype(jnp.float32),
    )

    def rotated(query_in, key_in, scale_in):
        return query_key(query_in, key_in, scale_in, cosine_table, sine_table)

    _, rot_pull = jax.vjp(rotated, q_raw, k_raw, attn_scale)
    q_raw_grad, k_raw_grad, scale_term = rot_pull((query_grad, key_grad.reshape(head_shape)))
    proj_grad = jnp.concatenate(
        [
            q_raw_grad.reshape(images, length, model_width),
            k_raw_grad.reshape(images, length, model_width),
            value_grad,
        ],
        axis=-1,
    ).astype(jnp.bfloat16)
    qkv_term = jnp.einsum("ild,ile->de", hidden_one, proj_grad, preferred_element_type=jnp.float32)
    hidden_one_grad = jnp.einsum(
        "ile,de->ild", proj_grad, qkv_full, preferred_element_type=jnp.float32
    )
    _, first_pull = jax.vjp(norm_mod, inputs, mod_one)
    input_part, mod_one_grad = first_pull(hidden_one_grad)
    tokens_grad = residual_grad + input_part
    image_one, image_two = lax.psum((mod_one_grad, mod_two_grad), "seq")
    cond_float = condition.astype(jnp.float32)
    condition_grad = jnp.dot(
        image_one, attn_mod_full.astype(jnp.float32).T, precision=finest
    ) + jnp.dot(image_two, ff_mod_full.astype(jnp.float32).T, precision=finest)
    attn_mod_term = jnp.dot(cond_float.T, mod_one_grad, precision=finest)
    ff_mod_term = jnp.dot(cond_float.T, mod_two_grad, precision=finest)
    scale_grad = lax.psum(scale_term, ("dp", "seq"))
    halves = (
        lax.psum_scatter(
            attn_mod_term.astype(jnp.bfloat16), "seq", scatter_dimension=0, tiled=True
        ).astype(jnp.float32),
        lax.psum_scatter(
            qkv_term.astype(jnp.bfloat16), "seq", scatter_dimension=0, tiled=True
        ).astype(jnp.float32),
        lax.psum_scatter(
            out_term.astype(jnp.bfloat16), "seq", scatter_dimension=0, tiled=True
        ).astype(jnp.float32),
        lax.psum_scatter(
            ff_mod_term.astype(jnp.bfloat16), "seq", scatter_dimension=0, tiled=True
        ).astype(jnp.float32),
        lax.psum_scatter(
            up_term.astype(jnp.bfloat16), "seq", scatter_dimension=0, tiled=True
        ).astype(jnp.float32),
        lax.psum_scatter(
            down_term.astype(jnp.bfloat16), "seq", scatter_dimension=0, tiled=True
        ).astype(jnp.float32),
    )
    shares = (
        lax.psum_scatter(halves[0], "dp", scatter_dimension=1, tiled=True),
        lax.psum_scatter(halves[1], "dp", scatter_dimension=1, tiled=True),
        lax.psum_scatter(halves[2], "dp", scatter_dimension=1, tiled=True),
        lax.psum_scatter(halves[3], "dp", scatter_dimension=1, tiled=True),
        lax.psum_scatter(halves[4], "dp", scatter_dimension=1, tiled=True),
        lax.psum_scatter(halves[5], "dp", scatter_dimension=1, tiled=True),
    )
    return (
        mixed,
        tokens_grad,
        condition_grad,
        shares[0],
        shares[1],
        scale_grad,
        shares[2],
        shares[3],
        shares[4],
        shares[5],
    )


def solution(mesh):
    return jax.shard_map(
        shards,
        mesh=mesh,
        in_specs=(
            P("dp", "seq", None),
            P("dp", None),
            P("dp", None, "seq"),
            P("dp"),
            P(),
            P("dp", "seq", None),
            P("seq", None),
            P("seq", None),
            P(),
            P("seq", None),
            P("seq", None),
            P("seq", None),
            P("seq", None),
        ),
        out_specs=(
            P("dp", "seq", None),
            P("dp", "seq", None),
            P("dp", None),
            P("seq", "dp"),
            P("seq", "dp"),
            P(),
            P("seq", "dp"),
            P("seq", "dp"),
            P("seq", "dp"),
            P("seq", "dp"),
        ),
        check_vma=False,
    )
```

profile of v0, /device:TPU:0, one launch (start us, length us, event | category | flops | bytes accessed | tf_op | source)
XLA Modules:
  0.0 1173.2 jit_solution(6191023368959172980)
XLA Ops:
  9.9 12.2 %all-gather.9.cloned.1.call-done = bf16[768,1024]{1,0:T(8,128)(2,1)} async-done(((bf16[384,1024]{1,0:T(8,128)(2,1)}), bf16[768,1024]{1,0:T(8,128)(2,1)}) %all-gather.9.cloned.1.call-update) | async-done | bytes 1572880 | tf_op jit(solution)/shard_map/all_gather | solution.py:86
  23.9 17.8 %all-gather.11.cloned.1.call-done = bf16[1024,3072]{1,0:T(8,128)(2,1)} async-done(((bf16[512,3072]{1,0:T(8,128)(2,1)}), bf16[1024,3072]{1,0:T(8,128)(2,1)}) %all-gather.11.cloned.1.call-update) | async-done | bytes 6291472 | tf_op jit(solution)/shard_map/all_gather | solution.py:87
  41.6 4.7 fusion.10
  60.2 6.2 all-gather.13.cloned.1.call-done
  67.9 10.7 all-gather.15.cloned.1.call-done
  85.8 6.0 all-gather.17.cloned.1.call-done
  95.7 23.8 %all-gather.21.cloned.1.call-done = bf16[1024,6144]{1,0:T(8,128)(2,1)} async-done(((bf16[512,6144]{1,0:T(8,128)(2,1)}), bf16[1024,6144]{1,0:T(8,128)(2,1)}) %all-gather.21.cloned.1.call-update) | async-done | bytes 12582928 | tf_op jit(solution)/shard_map/all_gather | solution.py:90
  119.4 10.0 fusion.2
  129.4 9.5 all-gather.23.cloned.1.call-done
  138.9 13.9 %multiply_add_fusion = (f32[2,128,3072]{2,1,0:T(8,128)}, f32[2,128,3072]{2,1,0:T(8,128)S(1)}, f32[2,128,3072]{2,1,0:T(8,128)S(1)}) fusion(f32[2,128,6144]{2,1,0:T(8,128)} %fusion.2, bf16[3072,1024]{1,0:T(8,128)(2,1)} %all-gather.23.cloned.1.call-done, bf16[2,128,1024]{2,1,0:T(8,128)(2,1)} %param.18, f32[2]{0:T(128)} %fusion.67), kind=kOutput, calls=%fused_computation.26 | convolution fusion | flops 1668022272 | bytes 22544392 | tf_op jit(solution)/shard_map/ild,fd->ilf/dot_general | solution.py:152
  156.3 11.6 multiply_reduce_fusion.3
  175.0 4.4 multiply_reduce_fusion
  183.5 3.7 copy.89
  189.8 4.3 fusion.31
  202.2 3.5 bitcast_convert_fusion.3
  224.3 6.2 fusion.49
  235.9 4.6 bitcast_convert_fusion.1
  241.5 5.9 bitcast_convert_fusion.2
  247.5 9.7 bitcast_convert_fusion
  269.8 5.4 copy.99
  275.3 10.0 reduce-scatter.31.cloned.1.call-done
  285.3 5.4 copy.93
  290.8 19.5 %reduce-scatter.37.cloned.1.call-done = bf16[512,6144]{1,0:T(8,128)(2,1)} async-done(((bf16[1024,6144]{1,0:T(8,128)(2,1)}), bf16[512,6144]{1,0:T(8,128)(2,1)}) %reduce-scatter.37.cloned.1.call-update) | async-done | bytes 6291472 | tf_op jit(solution)/shard_map/reduce_scatter | solution.py:237
  310.3 9.0 convert_element_type.169
  320.0 5.5 fusion.42
  325.4 40.7 %psum.23 = f32[16]{0:T(128)} all-reduce(f32[16]{0:T(128)S(1)} %divide_multiply_fusion), channel_id=1, replica_groups=mesh['dp'=16,'seq'=2] {'dp','seq'}, use_global_device_ids=true, to_apply=%region_24.0 | all-reduce | flops 16 | bytes 128 | tf_op jit(solution)/shard_map/psum | solution.py:223
  376.8 65.2 %reduce-scatter.35.cloned.1.call-done = f32[384,64]{0,1:T(8,128)} async-done(((f32[384,1024]{0,1:T(8,128)}), f32[384,64]{0,1:T(8,128)}) %reduce-scatter.35.cloned.1.call-update) | async-done | bytes 98320 | tf_op jit(solution)/shard_map/reduce_scatter | solution.py:248
  442.0 82.4 %reduce-scatter.49.cloned.1.call-done = f32[64,512]{1,0:T(8,128)} async-done(((f32[1024,512]{1,0:T(8,128)}), f32[64,512]{1,0:T(8,128)}) %reduce-scatter.49.cloned.1.call-update) | async-done | bytes 131088
  524.4 127.6 %reduce-scatter.29.cloned.1.call-done = f32[384,64]{0,1:T(8,128)} async-done(((f32[384,1024]{0,1:T(8,128)}), f32[384,64]{0,1:T(8,128)}) %reduce-scatter.29.cloned.1.call-update) | async-done | bytes 98320 | tf_op jit(solution)/shard_map/reduce_scatter | solution.py:245
  652.0 151.8 %reduce-scatter.53.cloned.1.call-done = f32[64,1536]{1,0:T(8,128)} async-done(((f32[1024,1536]{1,0:T(8,128)}), f32[64,1536]{1,0:T(8,128)}) %reduce-scatter.53.cloned.1.call-update) | async-done | bytes 393232
  803.8 152.0 %reduce-scatter.47.cloned.1.call-done = f32[192,512]{1,0:T(8,128)} async-done(((f32[3072,512]{1,0:T(8,128)}), f32[192,512]{1,0:T(8,128)}) %reduce-scatter.47.cloned.1.call-update) | async-done | bytes 393232
  955.8 210.4 %reduce-scatter.39.cloned.1.call-done = f32[512,384]{1,0:T(8,128)} async-done(((f32[512,6144]{1,0:T(8,128)}), f32[512,384]{1,0:T(8,128)}) %reduce-scatter.39.cloned.1.call-update) | async-done | bytes 786448 | tf_op jit(solution)/shard_map/reduce_scatter | solution.py:249
  (226 shorter events, 104.5 us)
Async XLA Ops:
  7.2 15.0 %copy-start = (bf16[2,768]{1,0:T(2,128)(2,1)S(1)}, bf16[2,768]{1,0:T(2,128)(2,1)}, u32[]{:S(2)}) copy-start(bf16[2,768]{1,0:T(2,128)(2,1)} %param.14) | copy-start | bytes 9220
  7.2 14.9 %all-gather.9.cloned.1.call-start = ((), (), s32[]{:S(2)}) async-start(), calls=%async_computation.14 | async-start | bytes 2359296 | tf_op jit(solution)/shard_map/all_gather | solution.py:86
  8.0 33.7 %all-gather.11.cloned.1.call-start = ((), (), s32[]{:S(2)}) async-start(), calls=%async_computation.15 | async-start | bytes 9437184 | tf_op jit(solution)/shard_map/all_gather | solution.py:87
  8.7 49.7 %all-gather.19.cloned.1.call-start = ((), (), s32[]{:S(2)}) async-start(), calls=%async_computation.19 | async-start | bytes 2359296 | tf_op jit(solution)/shard_map/all_gather | solution.py:89
  9.4 57.0 %all-gather.13.cloned.1.call-start = ((), (), s32[]{:S(2)}) async-start(), calls=%async_computation.16 | async-start | bytes 1572864 | tf_op jit(solution)/shard_map/all_gather | solution.py:111
  9.7 36.6 %copy-start.41 = (f32[2,128]{1,0:T(2,128)}, f32[2,128]{1,0:T(2,128)S(1)}, u32[]{:S(2)}) copy-start(f32[2,128]{1,0:T(2,128)S(1)} %fusion.54) | copy-start | bytes 3076
  9.8 36.5 %copy-start.46 = (f32[2,128]{1,0:T(2,128)}, f32[2,128]{1,0:T(2,128)S(1)}, u32[]{:S(2)}) copy-start(f32[2,128]{1,0:T(2,128)S(1)} %fusion.68) | copy-start | bytes 3076
  9.8 42.5 %copy-start.44 = (f32[16]{0:T(128)}, f32[16]{0:T(128)S(1)}, u32[]{:S(2)}) copy-start(f32[16]{0:T(128)S(1)} %sqrt.4) | copy-start | bytes 196
  9.9 42.8 %copy-start.17 = (f32[2,128,16,8]{1,3,2,0:T(8,128)}, f32[2,128,16,8]{1,3,2,0:T(8,128)S(1)}, u32[]{:S(2)}) copy-start(f32[2,128,16,8]{1,3,2,0:T(8,128)S(1)} %get-tuple-element.78) | copy-start | bytes 393220
  9.9 42.8 %copy-start.19 = (f32[2,128,16,8]{1,3,2,0:T(8,128)}, f32[2,128,16,8]{1,3,2,0:T(8,128)S(1)}, u32[]{:S(2)}) copy-start(f32[2,128,16,8]{1,3,2,0:T(8,128)S(1)} %get-tuple-element.79) | copy-start | bytes 393220
  23.9 22.5 %copy-start.38 = (f32[2,1024]{1,0:T(2,128)}, f32[2,1024]{1,0:T(2,128)S(1)}, u32[]{:S(2)}) copy-start(f32[2,1024]{1,0:T(2,128)S(1)} %convolution_add_fusion.1) | copy-start | bytes 24580
  51.5 27.1 %all-gather.15.cloned.1.call-start = ((), (), s32[]{:S(2)}) async-start(), calls=%async_computation.17 | async-start | bytes 1572864 | tf_op jit(solution)/shard_map/all_gather | solution.py:110
  55.4 36.4 %all-gather.17.cloned.1.call-start = ((), (), s32[]{:S(2)}) async-start(), calls=%async_computation.18 | async-start | bytes 3145728 | tf_op jit(solution)/shard_map/all_gather | solution.py:88
  56.0 63.5 %all-gather.21.cloned.1.call-start = ((), (), s32[]{:S(2)}) async-start(), calls=%async_computation.20 | async-start | bytes 18874368 | tf_op jit(solution)/shard_map/all_gather | solution.py:90
  56.7 82.2 %all-gather.23.cloned.1.call-start = ((), (), s32[]{:S(2)}) async-start(), calls=%async_computation.21 | async-start | bytes 9437184 | tf_op jit(solution)/shard_map/all_gather | solution.py:91
  57.5 152.9 %reduce-scatter.43.cloned.1.call-start = ((), (), s32[]{:S(2)}) async-start(), calls=%async_computation.30 | async-start | bytes 1572864
  189.7 34.6 %reduce-scatter.27.cloned.1.call-start = ((), (), s32[]{:S(2)}) async-start(), calls=%async_computation.22 | async-start | bytes 1572864 | tf_op jit(solution)/shard_map/reduce_scatter | solution.py:191
  196.3 60.9 %reduce-scatter.51.cloned.1.call-start = ((), (), s32[]{:S(2)}) async-start(), calls=%async_computation.34 | async-start | bytes 2359296
  201.7 60.3 %reduce-scatter.33.cloned.1.call-start = ((), (), s32[]{:S(2)}) async-start(), calls=%async_computation.25 | async-start | bytes 3145728 | tf_op jit(solution)/shard_map/reduce_scatter | solution.py:231
  205.7 59.3 %reduce-scatter.45.cloned.1.call-start = ((), (), s32[]{:S(2)}) async-start(), calls=%async_computation.31 | async-start | bytes 2359296
  235.8 34.0 %reduce-scatter.41.cloned.1.call-start = ((), (), s32[]{:S(2)}) async-start(), calls=%async_computation.29 | async-start | bytes 9437184 | tf_op jit(solution)/shard_map/reduce_scatter | solution.py:240
  240.5 44.9 %reduce-scatter.31.cloned.1.call-start = ((), (), s32[]{:S(2)}) async-start(), calls=%async_computation.24 | async-start | bytes 9437184 | tf_op jit(solution)/shard_map/reduce_scatter | solution.py:228
  247.4 62.9 %reduce-scatter.37.cloned.1.call-start = ((), (), s32[]{:S(2)}) async-start(), calls=%async_computation.27 | async-start | bytes 18874368 | tf_op jit(solution)/shard_map/reduce_scatter | solution.py:237
  257.2 184.8 %reduce-scatter.35.cloned.1.call-start = ((), (), s32[]{:S(2)}) async-start(), calls=%async_computation.26 | async-start | bytes 1671168 | tf_op jit(solution)/shard_map/reduce_scatter | solution.py:248
  262.0 262.4 %reduce-scatter.49.cloned.1.call-start = ((), (), s32[]{:S(2)}) async-start(), calls=%async_computation.33 | async-start | bytes 2228224
  264.9 387.1 %reduce-scatter.29.cloned.1.call-start = ((), (), s32[]{:S(2)}) async-start(), calls=%async_computation.23 | async-start | bytes 1671168 | tf_op jit(solution)/shard_map/reduce_scatter | solution.py:245
  269.8 534.1 %reduce-scatter.53.cloned.1.call-start = ((), (), s32[]{:S(2)}) async-start(), calls=%async_computation.35 | async-start | bytes 6684672
  275.3 680.5 %reduce-scatter.47.cloned.1.call-start = ((), (), s32[]{:S(2)}) async-start(), calls=%async_computation.32 | async-start | bytes 6684672
  290.8 875.4 %reduce-scatter.39.cloned.1.call-start = ((), (), s32[]{:S(2)}) async-start(), calls=%async_computation.28 | async-start | bytes 13369344 | tf_op jit(solution)/shard_map/reduce_scatter | solution.py:249
  320.0 49.4 %copy-start.42 = (f32[2,128]{1,0:T(2,128)S(1)}, f32[2,128]{1,0:T(2,128)}, u32[]{:S(2)}) copy-start(f32[2,128]{1,0:T(2,128)} %copy-done.41) | copy-start | bytes 3076
  325.4 50.1 %copy-start.6 = (f32[2,128,1024]{2,1,0:T(8,128)S(1)}, f32[2,128,1024]{2,1,0:T(8,128)}, u32[]{:S(2)}) copy-start(f32[2,128,1024]{2,1,0:T(8,128)} %copy-done.5) | copy-start | bytes 3145732
  325.4 50.1 %copy-start.21 = (f32[2,128,1024]{2,1,0:T(8,128)S(1)}, f32[2,128,1024]{2,1,0:T(8,128)}, u32[]{:S(2)}) copy-start(f32[2,128,1024]{2,1,0:T(8,128)} %get-tuple-element.96) | copy-start | bytes 3145732
  (44 other events, 171.1 us)
Sparse Core Ops, SparseCore 0:
  9.6 12.4 all-gather.8
  23.7 17.9 all-gather.10
  43.2 10.9 all-gather.18
  56.2 10.1 all-gather.12
  68.4 10.1 all-gather.14
  80.0 11.7 all-gather.16
  93.3 26.0 all-gather.20
  121.0 17.9 all-gather.22
  189.8 9.6 reduce-scatter.42
  201.7 9.6 reduce-scatter.26
  213.7 10.1 reduce-scatter.50
  226.2 10.8 reduce-scatter.32
  239.2 10.2 reduce-scatter.44
  251.8 15.6 reduce-scatter.40
  269.7 15.6 reduce-scatter.30
  287.6 22.6 reduce-scatter.36
  316.2 125.6 reduce-scatter.34
  444.8 79.5 reduce-scatter.48
  530.5 121.4 reduce-scatter.28
  658.5 145.2 reduce-scatter.52
  810.5 145.2 reduce-scatter.46
  962.9 203.1 reduce-scatter.38
where the time goes:
time: 1180 us; the launch traced here: 1170 us
  waiting for transfers between devices  909 us (77%)
  matrix products  112 us (9%)
  local copies, waits for them, and re-layouts  56.2 us (5%)
  blocking collectives  44 us (4%)
  other arithmetic  34.1 us (3%)
  between operations  15.4 us (1%)
    unnamed x28, waiting for transfers between devices  390 us
    reduce_scatter x1, waiting for transfers between devices, shards(): lax.psum_scatter(halves[4], 'dp', scatter_dimension=1, tiled=True)  210 us
    reduce_scatter x1, waiting for transfers between devices, shards(): lax.psum_scatter(halves[0], 'dp', scatter_dimension=1, tiled=True)  128 us
    reduce_scatter x1, waiting for transfers between devices, shards(): lax.psum_scatter(halves[3], 'dp', scatter_dimension=1, tiled=True)  65.2 us
    unnamed x119, local copies, waits for them, and re-layouts  42.4 us
    psum x1, blocking collectives, shards(): scale_grad = lax.psum(scale_term, ('dp', 'seq'))  40.7 us
    all_gather x1, waiting for transfers between devices, shards(): lax.all_gather(up_weight, 'seq', axis=0, tiled=True)  23.8 us
  transfers between devices with their start and end apart: 22, of which 15 were waited for; matrix products, arithmetic and copies ran while one was open for 12% of the time, Pallas kernels for 0%

commit v1 on v0

v1 whole, which is shorter than its diff:
```python
import math

import jax
import jax.numpy as jnp
import numpy as np
from jax import lax
from jax.experimental import pallas as pl
from jax.experimental.pallas import tpu as pltpu
from jax.sharding import PartitionSpec as P

HEAD_DIM = 64
GRID = 16
EPS = 1e-06
BF = jnp.bfloat16
F32 = jnp.float32
FINEST = lax.Precision.HIGHEST
LANES = 256
VMEM = 56 * 1024 * 1024


def nn(a, b):
    return lax.dot_general(a, b, (((1,), (0,)), ((), ())), preferred_element_type=F32)


def nt(a, b):
    return lax.dot_general(a, b, (((1,), (1,)), ((), ())), preferred_element_type=F32)


def tn(a, b):
    return lax.dot_general(a, b, (((0,), (0,)), ((), ())), preferred_element_type=F32)


def angle_constants(heads):
    quarter = HEAD_DIM // 8
    counter = np.arange(quarter)[None, :] * heads + np.arange(heads)[:, None]
    freq = (math.pi * np.power(10.0, counter / (heads * quarter))).astype(np.float32)
    coords = ((2.0 * np.arange(GRID) + 1.0) / GRID - 1.0).astype(np.float32)
    angles = (coords[:, None, None] * freq[None]).astype(np.float32).astype(np.float64)
    cos, sin = np.cos(angles), np.sin(angles)
    table = np.zeros((3, 2, GRID, heads, HEAD_DIM))
    q = quarter
    for part in range(2):
        lo = part * q
        table[0, part, :, :, lo : lo + q] = cos
        table[0, part, :, :, 2 * q + lo : 3 * q + lo] = cos
        table[1, part, :, :, lo : lo + q] = -sin
        table[2, part, :, :, 2 * q + lo : 3 * q + lo] = sin
    table[0, 0, :, :, 4 * q :] = 1.0
    return table.reshape(3, 2 * GRID, heads * HEAD_DIM).astype(np.float32)


def segment_matrix():
    rows = lax.broadcasted_iota(jnp.int32, (LANES, LANES), 0) // HEAD_DIM
    cols = lax.broadcasted_iota(jnp.int32, (LANES, LANES), 1) // HEAD_DIM
    return (rows == cols).astype(F32).astype(BF)


def segment_sum(values, ones):
    high = values.astype(BF)
    low = (values - high.astype(F32)).astype(BF)
    return nn(high, ones) + nn(low, ones)


def tables_of(onehot, table):
    return [
        lax.dot_general(
            onehot, table[i], (((1,), (0,)), ((), ())), precision=FINEST, preferred_element_type=F32
        )
        for i in range(3)
    ]


def spin(values, tabs, sign):
    cos, first, second = tabs
    q = HEAD_DIM // 4
    turned = pltpu.roll(values, LANES - q, 1) * first + pltpu.roll(values, q, 1) * second
    return values * cos + sign * turned


def head_masks():
    lane = lax.broadcasted_iota(jnp.int32, (1, LANES), 1) // HEAD_DIM
    return [lane == h for h in range(LANES // HEAD_DIM)]


def halves(core, values):
    half = values.shape[1] // 2
    a, b = values[:, :half], values[:, half:]
    return jnp.where(core == 0, a, b), jnp.where(core == 0, b, a)


def whole_of(core, own, other):
    return jnp.concatenate(
        [jnp.where(core == 0, own, other), jnp.where(core == 0, other, own)], axis=1
    )


def normed(values):
    scale = lax.rsqrt(jnp.mean(values * values, axis=-1, keepdims=True) + EPS)
    return values * scale, scale


def norm_back(unit, scale, mod, grad):
    inner = grad * (1.0 + mod)
    into = scale * (inner - unit * jnp.mean(inner * unit, axis=-1, keepdims=True))
    return into, jnp.sum(grad * unit, axis=0, keepdims=True)


def forward_kernel(
    place, x_ref, mod_ref, hot_ref, tab_ref, root_ref, qo, ko, vo, qp, kp, vp,
    q_out, k_out, v_out, att_out, own_out, other_out, own_ref, other_ref,
):
    core = place[0]

    @pl.when(pl.program_id(0) == 0)
    def _():
        unit, _ = normed(x_ref[...].astype(F32))
        own, other = halves(core, (unit * (1.0 + mod_ref[...])).astype(BF))
        own_ref[...] = own
        other_ref[...] = other
        own_out[...] = own
        other_out[...] = other

    own, other = own_ref[...], other_ref[...]
    q = nn(own, qo[...]) + nn(other, qp[...])
    k = nn(own, ko[...]) + nn(other, kp[...])
    v = (nn(own, vo[...]) + nn(other, vp[...])).astype(BF)
    q_out[...] = q
    k_out[...] = k
    v_out[...] = v
    ones = segment_matrix()
    tabs = tables_of(hot_ref[...], tab_ref)
    root = root_ref[...]
    qr = spin(q * (lax.rsqrt(segment_sum(q * q, ones) + EPS) * root), tabs, 1.0).astype(BF)
    kr = spin(k * (lax.rsqrt(segment_sum(k * k, ones) + EPS) * root), tabs, 1.0).astype(BF)
    total = jnp.zeros(q.shape, F32)
    zero = jnp.zeros_like(qr)
    for mask in head_masks():
        scores = nt(jnp.where(mask, qr, zero), kr)
        expo = jnp.exp(scores - jnp.max(scores, axis=-1, keepdims=True))
        prob = (expo / jnp.sum(expo, axis=-1, keepdims=True)).astype(BF)
        total = jnp.where(mask, nn(prob, v), total)
    att_out[...] = total.astype(BF)


def feed_kernel(
    place, scale_ref, x_ref, att_ref, mod_ref, og_ref, wo_ref, wp_ref, ao, ap, go, gp, do, dp,
    mixed_out, rgrad_out, rlow_out, mgrad_out, own_out, other_out, act_out, gu_out,
    res_ref, own_ref, other_ref, cot_ref, mix_ref, hgo_ref, hgp_ref,
):
    core = place[0]
    step = pl.program_id(0)
    steps = pl.num_programs(0)
    block = ao.shape[1]

    @pl.when(step == 0)
    def _():
        att_own, att_other = halves(core, att_ref[...])
        residual = (
            x_ref[...].astype(F32) + nn(att_own, wo_ref[...]) + nn(att_other, wp_ref[...])
        )
        res_ref[...] = residual
        unit, _ = normed(residual)
        own, other = halves(core, (unit * (1.0 + mod_ref[...])).astype(BF))
        own_ref[...] = own
        other_ref[...] = other
        own_out[...] = own
        other_out[...] = other
        cot_ref[...] = (og_ref[...].astype(F32) * scale_ref[0, 0]).astype(BF)
        mix_ref[...] = jnp.zeros_like(mix_ref)
        hgo_ref[...] = jnp.zeros_like(hgo_ref)
        hgp_ref[...] = jnp.zeros_like(hgp_ref)

    own, other = own_ref[...], other_ref[...]
    a = nn(own, ao[...]) + nn(other, ap[...])
    g = nn(own, go[...]) + nn(other, gp[...])
    down = jnp.where((step * 2 >= steps) == (core == 1), do[...], dp[...])
    phi = 0.5 * (1.0 + lax.erf(g * (1.0 / math.sqrt(2.0))))
    gelu = g * phi
    act = (a * gelu).astype(BF)
    act_out[...] = act
    mix_ref[...] += nn(act, down)
    act_grad = nt(cot_ref[...], down)
    a_grad = (act_grad * gelu).astype(BF)
    slope = phi + g * (jnp.exp(-0.5 * g * g) * (1.0 / math.sqrt(2.0 * math.pi)))
    g_grad = (act_grad * a * slope).astype(BF)
    at = pl.multiple_of(step * block, block)
    gu_out[:, pl.ds(at, block)] = a_grad
    gu_out[:, pl.ds(pl.multiple_of(steps * block + step * block, block), block)] = g_grad
    hgo_ref[...] += nt(a_grad, ao[...]) + nt(g_grad, go[...])
    hgp_ref[...] += nt(a_grad, ap[...]) + nt(g_grad, gp[...])

    @pl.when(step == steps - 1)
    def _():
        residual = res_ref[...]
        mixed_out[...] = (residual + mix_ref[...]).astype(BF)
        unit, scale = normed(residual)
        into, mgrad = norm_back(
            unit, scale, mod_ref[...], whole_of(core, hgo_ref[...], hgp_ref[...])
        )
        mgrad_out[...] = mgrad
        total = og_ref[...].astype(F32) * scale_ref[0, 0] + into
        rgrad_out[...] = total
        rlow_out[...] = total.astype(BF)


def backward_kernel(
    place, x_ref, mod_ref, hot_ref, tab_ref, root_ref, rgrad_ref, rlow_ref, wo_ref, wp_ref,
    q_ref, k_ref, v_ref, qo, ko, vo, qp, kp, vp,
    qkv_out, scale_out, tgrad_out, mgrad_out, hgo_ref, hgp_ref,
):
    core = place[0]
    step = pl.program_id(0)
    steps = pl.num_programs(0)

    @pl.when(step == 0)
    def _():
        hgo_ref[...] = jnp.zeros_like(hgo_ref)
        hgp_ref[...] = jnp.zeros_like(hgp_ref)

    weight = jnp.where((step * 2 >= steps) == (core == 1), wo_ref[...], wp_ref[...])
    grad = nt(rlow_ref[...], weight).astype(BF)
    ones = segment_matrix()
    tabs = tables_of(hot_ref[...], tab_ref)
    root = root_ref[...]
    q, k, v = q_ref[...], k_ref[...], v_ref[...]
    q_inv = lax.rsqrt(segment_sum(q * q, ones) + EPS)
    k_inv = lax.rsqrt(segment_sum(k * k, ones) + EPS)
    qr = spin(q * (q_inv * root), tabs, 1.0).astype(BF)
    kr = spin(k * (k_inv * root), tabs, 1.0).astype(BF)
    dq = jnp.zeros(q.shape, F32)
    dk = jnp.zeros(q.shape, F32)
    dv = jnp.zeros(q.shape, F32)
    zero = jnp.zeros_like(qr)
    for mask in head_masks():
        scores = nt(kr, jnp.where(mask, qr, zero))
        expo = jnp.exp(scores - jnp.max(scores, axis=0, keepdims=True))
        prob = expo / jnp.sum(expo, axis=0, keepdims=True)
        pgrad = nt(v, jnp.where(mask, grad, zero))
        sgrad = (prob * (pgrad - jnp.sum(prob * pgrad, axis=0, keepdims=True))).astype(BF)
        dq = jnp.where(mask, tn(sgrad, kr), dq)
        dk = jnp.where(mask, nn(sgrad, qr), dk)
        dv = jnp.where(mask, nn(prob.astype(BF), grad), dv)
    dq = spin(dq, tabs, -1.0)
    dk = spin(dk, tabs, -1.0)
    q_scale, k_scale = q_inv * root, k_inv * root
    q_dot, k_dot = dq * q, dk * k
    scale_out[...] = jnp.sum(q_dot * q_scale + k_dot * k_scale, axis=0, keepdims=True)
    gq = (q_scale * (dq - q * (segment_sum(q_dot, ones) * (q_inv * q_inv)))).astype(BF)
    gk = (k_scale * (dk - k * (segment_sum(k_dot, ones) * (k_inv * k_inv)))).astype(BF)
    gv = dv.astype(BF)
    for i, part in enumerate((gq, gk, gv)):
        at = pl.multiple_of((i * steps + step) * LANES, LANES)
        qkv_out[:, pl.ds(at, LANES)] = part
    hgo_ref[...] += nt(gq, qo[...]) + nt(gk, ko[...]) + nt(gv, vo[...])
    hgp_ref[...] += nt(gq, qp[...]) + nt(gk, kp[...]) + nt(gv, vp[...])

    @pl.when(step == steps - 1)
    def _():
        unit, scale = normed(x_ref[...].astype(F32))
        into, mgrad = norm_back(
            unit, scale, mod_ref[...], whole_of(core, hgo_ref[...], hgp_ref[...])
        )
        mgrad_out[...] = mgrad
        tgrad_out[...] = rgrad_ref[...] + into


def weight_kernel(place, bo, bp, ao, ap, send_a, keep_a, send_b, keep_b):
    one, two = place[1], place[2]
    total = tn(bo[...], ao[...]) + tn(bp[...], ap[...])
    cell = total.shape[0] // 4
    half = total.shape[1] // 2
    cells = [total[i * cell : (i + 1) * cell] for i in range(4)]
    for i in range(2):
        zero, unit = cells[2 * i][:, :half], cells[2 * i + 1][:, :half]
        send_a[0, i] = jnp.where(one == 0, unit, zero).astype(BF)
        keep_a[0, i] = jnp.where(one == 0, zero, unit).astype(BF)
        zero, unit = cells[i][:, half:], cells[2 + i][:, half:]
        send_b[0, i] = jnp.where(two == 0, unit, zero).astype(BF)
        keep_b[0, i] = jnp.where(two == 0, zero, unit).astype(BF)


def full(shape):
    return pl.BlockSpec(shape, lambda *_: (0,) * len(shape))


def call(kernel, grid, place, args, specs, outs, out_specs, scratch, flops, moved, exps=0):
    return pl.pallas_call(
        kernel,
        out_shape=outs,
        grid_spec=pltpu.PrefetchScalarGridSpec(
            num_scalar_prefetch=1,
            grid=grid,
            in_specs=specs,
            out_specs=out_specs,
            scratch_shapes=scratch,
        ),
        compiler_params=pltpu.CompilerParams(vmem_limit_bytes=VMEM),
        cost_estimate=pl.CostEstimate(
            flops=int(flops), bytes_accessed=int(moved), transcendentals=int(exps)
        ),
    )(place, *args)


def struct(shape, dtype):
    return jax.ShapeDtypeStruct(shape, dtype)


def shards(n, tokens, condition, positions, weight_codes, loss_table, out_grad, mod_attn,
           qkv_weight, attn_scale, out_weight, mod_ff, up_weight, down_weight):
    images, part, width = tokens.shape
    rows = images * part
    heads = attn_scale.shape[0]
    ff = 2 * down_weight.shape[0]
    low = 1 if n <= 16 else n // 4
    high = n // (4 * low)
    me = lax.axis_index("dp")
    core = lax.axis_index("seq")
    one = (me // low) % 2
    two = (me // (2 * low)) % 2
    place = jnp.stack([core, one, two]).astype(jnp.int32)

    def swap(values):
        return lax.ppermute(values, "seq", [(0, 1), (1, 0)])

    def cross(values, stride):
        return lax.ppermute(
            values, "dp", [(i, i + stride - 2 * stride * ((i // stride) % 2)) for i in range(n)]
        )

    def pick(values, index, axis=0):
        return lax.dynamic_index_in_dim(values, index, axis, keepdims=False)

    x = jnp.concatenate([pick(tokens, core), swap(pick(tokens, 1 - core))], axis=0)
    pos = jnp.concatenate([pick(positions, core), swap(pick(positions, 1 - core))], axis=1)
    mods = jnp.concatenate([mod_attn, mod_ff], axis=1)
    cond_rows = mod_attn.shape[0]
    cond_own = lax.dynamic_slice_in_dim(condition, core * cond_rows, cond_rows, 1)
    mod_part = jnp.dot(cond_own, mods, preferred_element_type=F32)
    mod_mine = pick(mod_part, core) + swap(pick(mod_part, 1 - core))
    mod_one, mod_two = mod_mine[None, :width], mod_mine[None, width:]
    qkv_other = swap(qkv_weight)
    out_other = swap(out_weight)
    og = jnp.concatenate([pick(out_grad, core), swap(pick(out_grad, 1 - core))], axis=0)
    late_up, late_down, qkv_other = lax.optimization_barrier((up_weight, down_weight, qkv_other))
    up_other = swap(late_up)
    down_other = swap(late_down)

    cells = lax.broadcasted_iota(jnp.int32, (rows, GRID), 1)
    onehot = jnp.concatenate(
        [(pos[0][:, None] == cells).astype(F32), (pos[1][:, None] == cells).astype(F32)], axis=1
    )
    table = jnp.asarray(angle_constants(heads))
    root = jnp.repeat(jnp.sqrt(attn_scale), HEAD_DIM)[None, :]

    steps = width // LANES
    half = width // 2
    col = pl.BlockSpec((rows, LANES), lambda j, p: (0, j))
    shared = [
        full((rows, width)),
        full((1, width)),
        full((rows, 2 * GRID)),
        pl.BlockSpec((3, 2 * GRID, LANES), lambda j, p: (0, 0, j)),
        pl.BlockSpec((1, LANES), lambda j, p: (0, j)),
    ]
    qkv_specs = [
        pl.BlockSpec((half, LANES), lambda j, p, i=i: (0, i * steps + j)) for i in (0, 1, 2, 0, 1, 2)
    ]
    qkv_args = [qkv_weight] * 3 + [qkv_other] * 3
    q_raw, k_raw, value, attended, h1_own, h1_other = call(
        forward_kernel,
        (steps,),
        place,
        [x, mod_one, onehot, table, root] + qkv_args,
        shared + qkv_specs,
        [struct((rows, width), F32)] * 2 + [struct((rows, width), BF)] * 2 + [struct((rows, half), BF)] * 2,
        [col] * 4 + [full((rows, half))] * 2,
        [pltpu.VMEM((rows, half), BF)] * 2,
        8 * rows * width * width,
        8 * width * width + 8 * rows * width * 2,
        heads * rows * rows,
    )

    levels = loss_table.shape[0]
    picked = (weight_codes[:, None] == jnp.arange(levels)[None, :]).astype(F32)
    image_scale = pick(jnp.sum(picked * loss_table[None, :], axis=1), core)
    cot_low = (og.astype(F32) * image_scale).astype(BF)
    block = 512
    count = ff // block
    up_specs = [
        pl.BlockSpec((half, block), lambda j, p, i=i: (0, i * count + j)) for i in (0, 0, 1, 1)
    ]
    down_specs = [
        pl.BlockSpec(
            (block, width),
            lambda j, p: (jnp.clip(j - p[0] * (count // 2), 0, count // 2 - 1), 0),
        ),
        pl.BlockSpec(
            (block, width),
            lambda j, p: (jnp.clip(j - (1 - p[0]) * (count // 2), 0, count // 2 - 1), 0),
        ),
    ]
    mixed_mine, res_grad, res_low, mod_two_grad, h2_own, h2_other, act, gate_up = call(
        feed_kernel,
        (count,),
        place,
        [image_scale.reshape(1, 1), x, attended, mod_two, og, out_weight, out_other]
        + [up_weight, up_other, up_weight, up_other, down_weight, down_other],
        [
            pl.BlockSpec(memory_space=pltpu.SMEM),
            full((rows, width)),
            full((rows, width)),
            full((1, width)),
            full((rows, width)),
            full((half, width)),
            full((half, width)),
        ]
        + up_specs
        + down_specs,
        [
            struct((rows, width), BF),
            struct((rows, width), F32),
            struct((rows, width), BF),
            struct((1, width), F32),
            struct((rows, half), BF),
            struct((rows, half), BF),
            struct((rows, ff), BF),
            struct((rows, 2 * ff), BF),
        ],
        [
            full((rows, width)),
            full((rows, width)),
            full((rows, width)),
            full((1, width)),
            full((rows, half)),
            full((rows, half)),
            pl.BlockSpec((rows, block), lambda j, p: (0, j)),
            full((rows, 2 * ff)),
        ],
        [
            pltpu.VMEM((rows, width), F32),
            pltpu.VMEM((rows, half), BF),
            pltpu.VMEM((rows, half), BF),
            pltpu.VMEM((rows, width), BF),
            pltpu.VMEM((rows, width), F32),
            pltpu.VMEM((rows, half), F32),
            pltpu.VMEM((rows, half), F32),
        ],
        2 * rows * width * (width + 6 * ff),
        2 * width * (width + 3 * ff) + 12 * rows * ff,
        2 * rows * ff,
    )

    def weight_grad(cols_own, cols_other, rows_own, rows_other):
        cols = cols_own.shape[1]
        depth = rows_other.shape[1]
        cell = cols // (4 * high)
        at = 0 if rows_own.shape[1] == depth else 1
        outs = [struct((high, 2, cell, depth // 2), BF)] * 4
        return call(
            weight_kernel,
            (high,),
            place,
            [cols_own, cols_other, rows_own, rows_other],
            [pl.BlockSpec((rows, 4 * cell), lambda j, p: (0, j))] * 2
            + [
                pl.BlockSpec((rows, depth), lambda j, p: (0, at * p[0])),
                full((rows, depth)),
            ],
            outs,
            [pl.BlockSpec((1, 2, cell, depth // 2), lambda j, p: (j, 0, 0, 0))] * 4,
            [],
            4 * rows * cols * depth,
            4 * rows * (cols + depth) + 2 * cols * depth,
        )

    def plane_sum(parts):
        send_a, keep_a, send_b, keep_b = parts
        got_a, got_b = cross(send_a, low), cross(send_b, 2 * low)

        def take(values, index):
            return lax.dynamic_index_in_dim(values, index, 1, keepdims=False).astype(F32)

        next_a = (take(keep_a, 1 - two) + take(got_a, 1 - two)).astype(BF)
        next_b = (take(keep_b, 1 - one) + take(got_b, 1 - one)).astype(BF)
        last_a, last_b = cross(next_a, 2 * low), cross(next_b, low)
        sum_a = take(keep_a, two) + take(got_a, two) + last_a.astype(F32)
        sum_b = take(keep_b, one) + take(got_b, one) + last_b.astype(F32)
        both = jnp.concatenate([sum_a, sum_b], axis=-1).astype(BF)
        return both.reshape(high * low, -1, both.shape[-1])

    lines = [
        [h * 4 * low + s * low + i for h in range(high) for i in range(low)] for s in range(4)
    ]

    def line_sum(values):
        return lax.psum_scatter(
            values, "dp", scatter_dimension=0, axis_index_groups=lines, tiled=False
        )

    def other_half(values):
        size = values.shape[1] // 2
        return swap(lax.dynamic_slice_in_dim(values, (1 - core) * size, size, 1))

    down_parts = weight_grad(cot_low, swap(cot_low), act, other_half(act))
    up_parts = weight_grad(gate_up, swap(gate_up), h2_own, swap(h2_other))
    out_parts = weight_grad(res_low, swap(res_low), attended, other_half(attended))

    weight_specs = [
        pl.BlockSpec(
            (LANES, width),
            lambda j, p: (jnp.clip(j - p[0] * (steps // 2), 0, steps // 2 - 1), 0),
        ),
        pl.BlockSpec(
            (LANES, width),
            lambda j, p: (jnp.clip(j - (1 - p[0]) * (steps // 2), 0, steps // 2 - 1), 0),
        ),
    ]
    qkv_grad, scale_lanes, tokens_mine, mod_one_grad = call(
        backward_kernel,
        (steps,),
        place,
        [x, mod_one, onehot, table, root, res_grad, res_low, out_weight, out_other]
        + [q_raw, k_raw, value]
        + qkv_args,
        shared
        + [full((rows, width)), full((rows, width))]
        + weight_specs
        + [col] * 3
        + qkv_specs,
        [
            struct((rows, 3 * width), BF),
            struct((1, width), F32),
            struct((rows, width), F32),
            struct((1, width), F32),
        ],
        [
            full((rows, 3 * width)),
            pl.BlockSpec((1, LANES), lambda j, p: (0, j)),
            full((rows, width)),
            full((1, width)),
        ],
        [pltpu.VMEM((rows, half), F32)] * 2,
        10 * rows * width * width,
        8 * width * width + 20 * rows * width,
        heads * rows * rows,
    )
    qkv_parts = weight_grad(qkv_grad, swap(qkv_grad), h1_own, swap(h1_other))

    down_sum = line_sum(plane_sum(down_parts))
    up_sum = line_sum(plane_sum(up_parts))
    out_plane, qkv_plane = plane_sum(out_parts), plane_sum(qkv_parts)
    last_sum = line_sum(jnp.concatenate([out_plane, qkv_plane], axis=1))
    out_cols = out_plane.shape[1]

    scale_term = jnp.sum(scale_lanes.reshape(heads, HEAD_DIM), axis=1) / (2.0 * attn_scale)
    both_rows = jnp.concatenate([mod_one_grad, mod_two_grad, scale_term[None, :]], axis=1)
    got_rows = swap(both_rows)
    pair = jnp.where(
        core == 0,
        jnp.concatenate([both_rows, got_rows], axis=0),
        jnp.concatenate([got_rows, both_rows], axis=0),
    )
    cond_part = jnp.dot(pair[:, : 2 * width], mods.astype(F32).T, precision=FINEST)
    cond_got = swap(cond_part)
    condition_grad = jnp.where(
        core == 0,
        jnp.concatenate([cond_part, cond_got], axis=1),
        jnp.concatenate([cond_got, cond_part], axis=1),
    )
    grads = pair[:, : 2 * width].reshape(images, 2, width)
    rest = jnp.concatenate([cond_own.astype(F32), pair[:, 2 * width :]], axis=1)
    stride = n // 2
    while stride:
        bit = (me // stride) % 2
        split = grads.reshape(grads.shape[0], 2, 2, -1)
        message = jnp.concatenate(
            [pick(split, 1 - bit, 2).reshape(grads.shape[0], -1), rest], axis=1
        )
        got = cross(message, stride)
        mine = pick(split, bit, 2).reshape(grads.shape[0], -1)
        wide = mine.shape[1]
        mine = jnp.concatenate([mine, rest], axis=1)
        every = jnp.where(
            bit == 0,
            jnp.concatenate([mine, got], axis=0),
            jnp.concatenate([got, mine], axis=0),
        )
        grads = every[:, :wide].reshape(every.shape[0], 2, -1)
        rest = every[:, wide:]
        stride //= 2
    cond_all = rest[:, :cond_rows]
    mod_attn_grad = jnp.dot(cond_all.T, grads[:, 0], precision=FINEST)
    mod_ff_grad = jnp.dot(cond_all.T, grads[:, 1], precision=FINEST)
    scale_grad = jnp.sum(rest[:, cond_rows:], axis=0)

    def home(values):
        got = swap(values[part:])
        own = values[:part]
        return jnp.where(core == 0, jnp.stack([own, got]), jnp.stack([got, own]))

    def turned(values):
        return values.astype(F32).T

    return (
        home(mixed_mine),
        home(tokens_mine),
        condition_grad,
        mod_attn_grad,
        turned(last_sum[out_cols:]),
        scale_grad,
        turned(last_sum[:out_cols]),
        mod_ff_grad,
        turned(up_sum),
        turned(down_sum),
    )


def solution(mesh):
    n = mesh.shape["dp"]

    def body(*args):
        return shards(n, *args)

    return jax.shard_map(
        body,
        mesh=mesh,
        in_specs=(
            P("dp", "seq", None),
            P("dp", None),
            P("dp", None, "seq"),
            P("dp"),
            P(),
            P("dp", "seq", None),
            P("seq", None),
            P("seq", None),
            P(),
            P("seq", None),
            P("seq", None),
            P("seq", None),
            P("seq", None),
        ),
        out_specs=(
            P("dp", "seq", None),
            P("dp", "seq", None),
            P("dp", None),
            P("seq", "dp"),
            P("seq", "dp"),
            P(),
            P("seq", "dp"),
            P("seq", "dp"),
            P("seq", "dp"),
            P("seq", "dp"),
        ),
        check_vma=False,
    )
```

time: 1180 us -> 310 us (0.26)
  waiting for transfers between devices: 909 us -> 124 us
  matrix products: 112 us -> 3.5 us
  Pallas kernels: 0 us -> 82.9 us
  blocking collectives: 44 us -> 0 us
  local copies, waits for them, and re-layouts: 56.2 us -> 19.6 us
  starting transfers between devices: 1.74 us -> 33.5 us
    reduce_scatter x8 -> x3, waiting for transfers between devices: 433 us -> 21.1 us  [line_sum(): lax.psum_scatter(values, 'dp', scatter_dimension=0, axis_index_groups=lin...]
    unnamed x28 -> x3, waiting for transfers between devices: 390 us -> 0.05 us
    dot_general x24 -> x4, matrix products: 112 us -> 3.5 us  [the longest x1 1.31 us: shards(): jnp.dot(pair[:, :2 * width], mods.astype(F32).T, precision=FINEST)]
    ppermute x0 -> x40, waiting for transfers between devices: none -> 103 us  [the longest x20 90.7 us: cross(): lax.ppermute(values, 'dp', [(i, i + stride - 2 * stride * (i // stride %...]
    all_gather x8 -> x0, waiting for transfers between devices: 86.2 us -> none  [the longest x1 23.8 us: shards(): lax.all_gather(up_weight, 'seq', axis=0, tiled=True)]
    pallas_call x0 -> x7, Pallas kernels: none -> 82.9 us  [call(): pl.pallas_call(kernel, out_shape=outs, grid_spec=pltpu.PrefetchScalarGrid...]
    psum x2 -> x0, blocking collectives: 44 us -> none  [the longest x1 40.7 us: shards(): scale_grad = lax.psum(scale_term, ('dp', 'seq'))]
    unnamed x119 -> x92, local copies, waits for them, and re-layouts: 42.4 us -> 5.99 us
  transfers between devices with their start and end apart: 22 -> 43, of which waited for: 15 -> 16; matrix products, arithmetic and copies ran while one was open for 12% -> 15% of each run, Pallas kernels for 0% -> 20%
where the time goes in v1:
time: 310 us; the launch traced here: 308 us
  waiting for transfers between devices  124 us (40%)
  Pallas kernels  82.9 us (27%)
  starting transfers between devices  33.5 us (11%)
  other arithmetic  30.4 us (10%)
  local copies, waits for them, and re-layouts  19.6 us (6%)
  between operations  14.5 us (5%)
  matrix products  3.5 us (1%)
    ppermute x20, waiting for transfers between devices, cross(): lax.ppermute(values, 'dp', [(i, i + stride - 2 * stride * (i // stride %...  90.7 us
    pallas_call x7, Pallas kernels, call(): pl.pallas_call(kernel, out_shape=outs, grid_spec=pltpu.PrefetchScalarGrid...  82.9 us
    ppermute x20, starting transfers between devices, cross(): lax.ppermute(values, 'dp', [(i, i + stride - 2 * stride * (i // stride %...  28.1 us
    reduce_scatter x3, waiting for transfers between devices, line_sum(): lax.psum_scatter(values, 'dp', scatter_dimension=0, axis_index_groups=lin...  21.1 us
    ppermute x20, waiting for transfers between devices, swap(): return lax.ppermute(values, 'seq', [(0, 1), (1, 0)])  12 us
  transfers between devices with their start and end apart: 43, of which 16 were waited for; matrix products, arithmetic and copies ran while one was open for 15% of the time, Pallas kernels for 20%

profile of v1, /device:TPU:0, one launch (start us, length us, event | category | flops | bytes accessed | tf_op | source)
XLA Modules:
  0.0 308.4 jit_solution(17830381411601649480)
XLA Ops:
  7.7 5.5 %collective-permute-done.3.qp.kp.vp = bf16[512,3072]{1,0:T(8,128)(2,1)S(1)} collective-permute-done((bf16[512,3072]{1,0:T(8,128)(2,1)}, bf16[512,3072]{1,0:T(8,128)(2,1)S(1)}, u32[]{:S(2)}, u32[]{:S(2)}) %collective-permute-start.3) | collective-permute-done | bytes 3145760 | tf_op jit(solution)/shard_map/ppermute | solution.py:323
  21.5 1.9 collective-permute-done.2
  24.6 3.3 %collective-permute-done.1 = f32[2048]{0:T(1024)S(1)} collective-permute-done((f32[2048]{0:T(1024)S(1)}, f32[2048]{0:T(1024)S(1)}, u32[]{:S(2)}, u32[]{:S(2)}) %collective-permute-start.1) | collective-permute-done | bytes 8224 | tf_op jit(solution)/shard_map/ppermute | solution.py:323
  31.1 13.5 %shard_map.213 = (f32[256,1024]{1,0:T(8,128)}, f32[256,1024]{1,0:T(8,128)}, bf16[256,1024]{1,0:T(8,128)(2,1)}, bf16[256,1024]{1,0:T(8,128)(2,1)}, bf16[256,512]{1,0:T(8,128)(2,1)}, /*index=5*/bf16[256,512]{1,0:T(8,128)(2,1)}) custom-call(s32[3]{0:T(128)} %pad_add_fusion.2.place, bf16[256,1024]{1,0:T(8,128)(2,1)} %pad_maximum_fusion.2.x_ref, ...), custom_call_target="tpu_custom_call" | custom-call | flops 2147483648 | bytes 12582912 | tf_op jit(solution)/shard_map/pallas_call | solution.py:287
  45.5 22.4 %shard_map.214 = (bf16[256,1024]{1,0:T(8,128)(2,1)}, f32[256,1024]{1,0:T(8,128)}, bf16[256,1024]{1,0:T(8,128)(2,1)}, f32[1,1024]{1,0:T(1,128)}, bf16[256,512]{1,...) custom-call(s32[3]{0:T(128)} %pad_add_fusion.2.place, ...), custom_call_target="tpu_custom_call" | custom-call | flops 10200547328 | bytes 30408704 | tf_op jit(solution)/shard_map/pallas_call | solution.py:287
  70.8 21.4 %shard_map.215 = (bf16[256,3072]{1,0:T(8,128)(2,1)}, f32[1,1024]{1,0:T(1,128)}, f32[256,1024]{1,0:T(8,128)}, f32[1,1024]{1,0:T(1,128)}) custom-call(s32[3]{0:T(128)} %pad_add_fusion.2.place, bf16[256,1024]{1,0:T(8,128)(2,1)} %pad_maximum_fusion.2.x_ref, f32[1,1024]{1,0:T(1,128)} %bitcast.137, f32[256,32]{1,0:T(8,128)} %concatenate.106.hot_ref, ...), custom_call_target="tpu_custom_call" | custom-call | flops 2684354560 | bytes 13631488 | tf_op jit(solution)/shard_map/pallas_call | solution.py:287
  96.0 6.0 %shard_map.219 = (bf16[4,2,64,768]{3,2,1,0:T(8,128)(2,1)}, bf16[4,2,64,768]{3,2,1,0:T(8,128)(2,1)}, bf16[4,2,64,768]{3,2,1,0:T(8,128)(2,1)}, bf16[4,2,64,768]{3,2,1,0:T(8,128)(2,1)}) custom-call(s32[3]{0:T(128)} %pad_add_fusion.2.place, bf16[256,1024]{1,0:T(8,128)(2,1)} %copy-done.23, bf16[256,1024]{1,0:T(8,128)(2,1)} %collective-permute-done.34.bp, ...), custom_call_target="tpu_custom_call" | custom-call | flops 1610612736 | bytes 5767168 | tf_op jit(solution)/shard_map/pallas_call | solution.py:287
  103.2 2.9 collective-permute-start.36
  106.9 4.9 %shard_map.216 = (bf16[4,2,64,256]{3,2,1,0:T(8,128)(2,1)}, bf16[4,2,64,256]{3,2,1,0:T(8,128)(2,1)}, bf16[4,2,64,256]{3,2,1,0:T(8,128)(2,1)}, bf16[4,2,64,256]{3,2,1,0:T(8,128)(2,1)}) custom-call(s32[3]{0:T(128)} %pad_add_fusion.2.place, bf16[256,1024]{1,0:T(8,128)(2,1)} %get-tuple-element.53.rlow_ref.bo, bf16[256,1024]{1,0:T(8,128)(2,1)} %collective-permute-done.16.bp, ...), custom_call_target="tpu_custom_call" | custom-call | flops 536870912 | bytes 2621440 | tf_op jit(solution)/shard_map/pallas_call | solution.py:287
  113.0 2.1 collective-permute-start.38
  115.8 13.8 %collective-permute-done.18 = bf16[4,2,64,256]{3,2,0,1:T(8,128)(2,1)S(1)} collective-permute-done((bf16[4,2,64,256]{3,2,0,1:T(8,128)(2,1)S(1)}, bf16[4,2,64,256]{3,2,0,1:T(8,128)(2,1)S(1)}, u32[]{:S(2)}, u32[]{:S(2)}) %collective-permute-start.18) | collective-permute-done | bytes 262176 | tf_op jit(solution)/shard_map/ppermute | solution.py:326
  131.1 1.8 collective-permute-start.20
  133.2 6.2 %shard_map.217 = (bf16[4,2,192,256]{3,2,1,0:T(8,128)(2,1)}, bf16[4,2,192,256]{3,2,1,0:T(8,128)(2,1)}, bf16[4,2,192,256]{3,2,1,0:T(8,128)(2,1)}, bf16[4,2,192,256]{3,2,1,0:T(8,128)(2,1)}) custom-call(s32[3]{0:T(128)} %pad_add_fusion.2.place, bf16[256,3072]{1,0:T(8,128)(2,1)} %get-tuple-element.65.bo, bf16[256,3072]{1,0:T(8,128)(2,1)} %collective-permute-done.22.bp, ...), custom_call_target="tpu_custom_call" | custom-call | flops 1610612736 | bytes 6815744 | tf_op jit(solution)/shard_map/pallas_call | solution.py:287
  140.7 1.8 collective-permute-start.24
  143.7 4.2 %collective-permute-done.37 = bf16[4,64,768]{2,1,0:T(8,128)(2,1)S(1)} collective-permute-done((bf16[4,64,768]{2,1,0:T(8,128)(2,1)S(1)}, bf16[4,64,768]{2,1,0:T(8,128)(2,1)S(1)}, u32[]{:S(2)}, u32[]{:S(2)}) %collective-permute-start.37) | collective-permute-done | bytes 393248 | tf_op jit(solution)/shard_map/ppermute | solution.py:326
  148.1 20.2 %collective-permute-done.39 = bf16[4,64,768]{2,1,0:T(8,128)(2,1)S(1)} collective-permute-done((bf16[4,64,768]{2,1,0:T(8,128)(2,1)S(1)}, bf16[4,64,768]{2,1,0:T(8,128)(2,1)S(1)}, u32[]{:S(2)}, u32[]{:S(2)}) %collective-permute-start.39) | collective-permute-done | bytes 393248 | tf_op jit(solution)/shard_map/ppermute | solution.py:326
  168.3 1.7 collective-permute-start.26
  171.7 1.7 collective-permute-start.21
  175.0 8.6 %shard_map.218 = (bf16[4,2,384,256]{3,2,1,0:T(8,128)(2,1)}, bf16[4,2,384,256]{3,2,1,0:T(8,128)(2,1)}, bf16[4,2,384,256]{3,2,1,0:T(8,128)(2,1)}, bf16[4,2,384,256]{3,2,1,0:T(8,128)(2,1)}) custom-call(s32[3]{0:T(128)} %pad_add_fusion.2.place, bf16[256,6144]{1,0:T(8,128)(2,1)} %get-tuple-element.72.bo, bf16[256,6144]{1,0:T(8,128)(2,1)} %collective-permute-done.28.bp, ...), custom_call_target="tpu_custom_call" | custom-call | flops 3221225472 | bytes 13107200 | tf_op jit(solution)/shard_map/pallas_call | solution.py:287
  185.3 6.3 %collective-permute-done.19 = bf16[4,64,256]{2,1,0:T(8,128)(2,1)S(1)} collective-permute-done((bf16[4,64,256]{2,1,0:T(8,128)(2,1)S(1)}, bf16[4,64,256]{2,1,0:T(8,128)(2,1)S(1)}, u32[]{:S(2)}, u32[]{:S(2)}) %collective-permute-start.19) | collective-permute-done | bytes 131104 | tf_op jit(solution)/shard_map/ppermute | solution.py:326
  195.0 1.8 collective-permute-start.32
  196.8 3.2 %collective-permute-done.25 = bf16[4,192,256]{2,1,0:T(8,128)(2,1)S(1)} collective-permute-done((bf16[4,192,256]{2,1,0:T(8,128)(2,1)S(1)}, bf16[4,192,256]{2,1,0:T(8,128)(2,1)S(1)}, u32[]{:S(2)}, u32[]{:S(2)}) %collective-permute-start.25) | collective-permute-done | bytes 393248 | tf_op jit(solution)/shard_map/ppermute | solution.py:326
  200.2 31.8 %collective-permute-done.27 = bf16[4,192,256]{2,1,0:T(8,128)(2,1)S(1)} collective-permute-done((bf16[4,192,256]{2,1,0:T(8,128)(2,1)S(1)}, bf16[4,192,256]{2,1,0:T(8,128)(2,1)S(1)}, u32[]{:S(2)}, u32[]{:S(2)}) %collective-permute-start.27) | collective-permute-done | bytes 393248 | tf_op jit(solution)/shard_map/ppermute | solution.py:326
  235.2 2.5 fusion.3
  239.3 2.6 collective-permute-start.12
  247.6 4.8 %collective-permute-done.31 = bf16[4,384,256]{2,1,0:T(8,128)(2,1)} collective-permute-done((bf16[4,384,256]{2,1,0:T(8,128)(2,1)}, bf16[4,384,256]{2,1,0:T(8,128)(2,1)}, u32[]{:S(2)}, u32[]{:S(2)}) %collective-permute-start.31) | collective-permute-done | bytes 786464 | tf_op jit(solution)/shard_map/ppermute | solution.py:326
  254.1 2.9 collective-permute-done.33
  256.9 1.7 fusion.1
  267.3 1.8 collective-permute-done.15
  273.6 1.7 convert_bitcast_fusion.1
  276.8 1.7 convert_bitcast_fusion.2
  278.5 21.1 %reduce-scatter.6.cloned.1.call-done = bf16[1,384,512]{2,1,0:T(8,128)(2,1)} async-done(((bf16[4,384,512]{2,1,0:T(8,128)(2,1)}), bf16[1,384,512]{2,1,0:T(8,128)(2,1)}) %reduce-scatter.6.cloned.1.call-update) | async-done | bytes 393232 | tf_op jit(solution)/shard_map/reduce_scatter | solution.py:496
  (256 shorter events, 66.1 us)
Async XLA Ops:
  7.2 266.4 %reduce-scatter.8.cloned.1.call-start = ((), (), s32[]{:S(2)}) async-start(), calls=%async_computation.5 | async-start | bytes 983040 | tf_op jit(solution)/shard_map/reduce_scatter | solution.py:496
  13.2 31.3 %collective-permute-start.6 = (bf16[512,6144]{1,0:T(8,128)(2,1)}, bf16[512,6144]{1,0:T(8,128)(2,1)}, u32[]{:S(2)}, u32[]{:S(2)}) collective-permute-start(bf16[512,6144]{1,0:T(8,128)(2,1)} %go.1), channel_id=1, source_target_pairs={{0,1},{1,0},{2,3},{3,2},{4,5},{5,4},{6,7},{7,6},{8,9},{9,8},{10,11... | collective-permute-start | bytes 18874376 | tf_op jit(solution)/shard_map/ppermute | solution.py:323
  13.6 30.9 %collective-permute-start.7 = (bf16[1536,1024]{1,0:T(8,128)(2,1)}, bf16[1536,1024]{1,0:T(8,128)(2,1)}, u32[]{:S(2)}, u32[]{:S(2)}) collective-permute-start(bf16[1536,1024]{1,0:T(8,128)(2,1)} %do.1), channel_id=1, source_target_pairs={{0,1},{1,0},{2,3},{3,2},{4,5},{5,4},{6,7},{7,6},{8,9},{9,8},{10,11... | collective-permute-start | bytes 9437192 | tf_op jit(solution)/shard_map/ppermute | solution.py:323
  23.4 21.1 %collective-permute-start.5 = (bf16[512,1024]{1,0:T(8,128)(2,1)S(1)}, bf16[512,1024]{1,0:T(8,128)(2,1)S(1)}, u32[]{:S(2)}, u32[]{:S(2)}) collective-permute-start(bf16[512,1024]{1,0:T(8,128)(2,1)S(1)} %copy-done.8), channel_id=1, source_target_pairs={{0,1},{1,0},{2,3},{3,2},{4,5},{5,4},{6,7},{7,6},{8,9},{9,8},{10,11... | collective-permute-start | bytes 3145736 | tf_op jit(solution)/shard_map/ppermute | solution.py:323
  69.1 26.0 %collective-permute-start.35 = (bf16[256,1536]{1,0:T(8,128)(2,1)S(1)}, bf16[256,1536]{1,0:T(8,128)(2,1)S(1)}, u32[]{:S(2)}, u32[]{:S(2)}) collective-permute-start(bf16[256,1536]{1,0:T(8,128)(2,1)S(1)} %constant_dynamic-slice_fusion), channel_id=1, source_target_pairs={{0,1},{1,0},{2,3},{3,2},{4,5},{5,4},{6,7},{7,6},{8,9},{9,8},{10,11... | collective-permute-start | bytes 2359304 | tf_op jit(solution)/shard_map/ppermute | solution.py:323
  70.2 24.6 %collective-permute-start.34 = (bf16[256,1024]{1,0:T(8,128)(2,1)S(1)}, bf16[256,1024]{1,0:T(8,128)(2,1)}, u32[]{:S(2)}, u32[]{:S(2)}) collective-permute-start(bf16[256,1024]{1,0:T(8,128)(2,1)S(1)} %multiply_convert_fusion.bo), channel_id=1, source_target_pairs={{0,1},{1,0},{2,3},{3,2},{4,5},{5,4},{6,7},{7,6},{8,9},{9,8},{10,11... | collective-permute-start | bytes 1572872 | tf_op jit(solution)/shard_map/ppermute | solution.py:323
  70.4 103.0 %collective-permute-start.28 = (bf16[256,6144]{1,0:T(8,128)(2,1)}, bf16[256,6144]{1,0:T(8,128)(2,1)}, u32[]{:S(2)}, u32[]{:S(2)}) collective-permute-start(bf16[256,6144]{1,0:T(8,128)(2,1)} %get-tuple-element.72.bo), channel_id=1, source_target_pairs={{0,1},{1,0},{2,3},{3,2},{4,5},{5,4},{6,7},{7,6},{8,9},{9,8},{10,11... | collective-permute-start | bytes 9437192 | tf_op jit(solution)/shard_map/ppermute | solution.py:323
  92.2 40.7 %collective-permute-start.22 = (bf16[256,3072]{1,0:T(8,128)(2,1)}, bf16[256,3072]{1,0:T(8,128)(2,1)}, u32[]{:S(2)}, u32[]{:S(2)}) collective-permute-start(bf16[256,3072]{1,0:T(8,128)(2,1)} %get-tuple-element.65.bo), channel_id=1, source_target_pairs={{0,1},{1,0},{2,3},{3,2},{4,5},{5,4},{6,7},{7,6},{8,9},{9,8},{10,11... | collective-permute-start | bytes 4718600 | tf_op jit(solution)/shard_map/ppermute | solution.py:323
  92.4 13.7 %collective-permute-start.16 = (bf16[256,1024]{1,0:T(8,128)(2,1)S(1)}, bf16[256,1024]{1,0:T(8,128)(2,1)}, u32[]{:S(2)}, u32[]{:S(2)}) collective-permute-start(bf16[256,1024]{1,0:T(8,128)(2,1)S(1)} %copy-done.20), channel_id=1, source_target_pairs={{0,1},{1,0},{2,3},{3,2},{4,5},{5,4},{6,7},{7,6},{8,9},{9,8},{10,11... | collective-permute-start | bytes 1572872 | tf_op jit(solution)/shard_map/ppermute | solution.py:323
  94.9 11.3 %collective-permute-start.17 = (bf16[256,512]{1,0:T(8,128)(2,1)S(1)}, bf16[256,512]{1,0:T(8,128)(2,1)S(1)}, u32[]{:S(2)}, u32[]{:S(2)}) collective-permute-start(bf16[256,512]{1,0:T(8,128)(2,1)S(1)} %constant_dynamic-slice_fusion.1), channel_id=1, source_target_pairs={{0,1},{1,0},{2,3},{3,2},{4,5},{5,4},{6,7},{7,6},{8,9},{9,8},{10,11... | collective-permute-start | bytes 786440 | tf_op jit(solution)/shard_map/ppermute | solution.py:323
  103.2 26.4 %collective-permute-start.36 = (bf16[4,2,64,768]{3,2,0,1:T(8,128)(2,1)S(1)}, bf16[4,2,64,768]{3,2,0,1:T(8,128)(2,1)S(1)}, u32[]{:S(2)}, u32[]{:S(2)}) collective-permute-start(bf16[4,2,64,768]{3,2,0,1:T(8,128)(2,1)S(1)} %copy.120), channel_id=1, source_target_pairs={{0,2},{2,0},{4,6},{6,4},{8,10},{10,8},{12,14},{14,12},{16,18},{18,... | collective-permute-start | bytes 2359304 | tf_op jit(solution)/shard_map/ppermute | solution.py:326
  112.9 16.7 %collective-permute-start.18 = (bf16[4,2,64,256]{3,2,0,1:T(8,128)(2,1)S(1)}, bf16[4,2,64,256]{3,2,0,1:T(8,128)(2,1)S(1)}, u32[]{:S(2)}, u32[]{:S(2)}) collective-permute-start(bf16[4,2,64,256]{3,2,0,1:T(8,128)(2,1)S(1)} %copy.102), channel_id=1, source_target_pairs={{0,2},{2,0},{4,6},{6,4},{8,10},{10,8},{12,14},{14,12},{16,18},{18,... | collective-permute-start | bytes 786440 | tf_op jit(solution)/shard_map/ppermute | solution.py:326
  113.0 27.6 %collective-permute-start.38 = (bf16[4,2,64,768]{3,2,0,1:T(8,128)(2,1)S(1)}, bf16[4,2,64,768]{3,2,0,1:T(8,128)(2,1)S(1)}, u32[]{:S(2)}, u32[]{:S(2)}) collective-permute-start(bf16[4,2,64,768]{3,2,0,1:T(8,128)(2,1)S(1)} %copy.123), channel_id=1, source_target_pairs={{0,4},{2,6},{4,0},{6,2},{8,12},{10,14},{12,8},{14,10},{16,20},{18,... | collective-permute-start | bytes 2359304 | tf_op jit(solution)/shard_map/ppermute | solution.py:326
  129.7 42.1 %collective-permute-start.29 = (bf16[256,512]{1,0:T(8,128)(2,1)}, bf16[256,512]{1,0:T(8,128)(2,1)}, u32[]{:S(2)}, u32[]{:S(2)}) collective-permute-start(bf16[256,512]{1,0:T(8,128)(2,1)} %get-tuple-element.74), channel_id=1, source_target_pairs={{0,1},{1,0},{2,3},{3,2},{4,5},{5,4},{6,7},{7,6},{8,9},{9,8},{10,11... | collective-permute-start | bytes 786440 | tf_op jit(solution)/shard_map/ppermute | solution.py:323
  131.1 11.4 %collective-permute-start.20 = (bf16[4,2,64,256]{3,2,0,1:T(8,128)(2,1)S(1)}, bf16[4,2,64,256]{3,2,0,1:T(8,128)(2,1)S(1)}, u32[]{:S(2)}, u32[]{:S(2)}) collective-permute-start(bf16[4,2,64,256]{3,2,0,1:T(8,128)(2,1)S(1)} %copy.105), channel_id=1, source_target_pairs={{0,4},{2,6},{4,0},{6,2},{8,12},{10,14},{12,8},{14,10},{16,20},{18,... | collective-permute-start | bytes 786440 | tf_op jit(solution)/shard_map/ppermute | solution.py:326
  132.9 15.0 %collective-permute-start.37 = (bf16[4,64,768]{2,1,0:T(8,128)(2,1)S(1)}, bf16[4,64,768]{2,1,0:T(8,128)(2,1)S(1)}, u32[]{:S(2)}, u32[]{:S(2)}) collective-permute-start(bf16[4,64,768]{2,1,0:T(8,128)(2,1)S(1)} %fusion.12), channel_id=1, source_target_pairs={{0,4},{2,6},{4,0},{6,2},{8,12},{10,14},{12,8},{14,10},{16,20},{18,... | collective-permute-start | bytes 1179656 | tf_op jit(solution)/shard_map/ppermute | solution.py:326
  140.7 30.5 %collective-permute-start.24 = (bf16[4,2,192,256]{3,2,0,1:T(8,128)(2,1)S(1)}, bf16[4,2,192,256]{3,2,0,1:T(8,128)(2,1)S(1)}, u32[]{:S(2)}, u32[]{:S(2)}) collective-permute-start(bf16[4,2,192,256]{3,2,0,1:T(8,128)(2,1)S(1)} %copy.108), channel_id=1, source_target_pairs={{0,2},{2,0},{4,6},{6,4},{8,10},{10,8},{12,14},{14,12},{16,18},{18,... | collective-permute-start | bytes 2359304 | tf_op jit(solution)/shard_map/ppermute | solution.py:326
  142.6 25.7 %collective-permute-start.39 = (bf16[4,64,768]{2,1,0:T(8,128)(2,1)S(1)}, bf16[4,64,768]{2,1,0:T(8,128)(2,1)S(1)}, u32[]{:S(2)}, u32[]{:S(2)}) collective-permute-start(bf16[4,64,768]{2,1,0:T(8,128)(2,1)S(1)} %fusion.14), channel_id=1, source_target_pairs={{0,2},{2,0},{4,6},{6,4},{8,10},{10,8},{12,14},{14,12},{16,18},{18,... | collective-permute-start | bytes 1179656 | tf_op jit(solution)/shard_map/ppermute | solution.py:326
  147.9 86.3 %collective-permute-start.10 = (f32[1,2064]{1,0:T(1,128)}, f32[1,2064]{1,0:T(1,128)}, u32[]{:S(2)}, u32[]{:S(2)}) collective-permute-start(f32[1,2064]{1,0:T(1,128)} %pad_maximum_fusion.8), channel_id=1, source_target_pairs={{0,1},{1,0},{2,3},{3,2},{4,5},{5,4},{6,7},{7,6},{8,9},{9,8},{10,11... | collective-permute-start | bytes 24776 | tf_op jit(solution)/shard_map/ppermute | solution.py:323
  168.3 25.0 %collective-permute-start.26 = (bf16[4,2,192,256]{3,2,0,1:T(8,128)(2,1)S(1)}, bf16[4,2,192,256]{3,2,0,1:T(8,128)(2,1)}, u32[]{:S(2)}, u32[]{:S(2)}) collective-permute-start(bf16[4,2,192,256]{3,2,0,1:T(8,128)(2,1)S(1)} %copy.111), channel_id=1, source_target_pairs={{0,4},{2,6},{4,0},{6,2},{8,12},{10,14},{12,8},{14,10},{16,20},{18,... | collective-permute-start | bytes 2359304 | tf_op jit(solution)/shard_map/ppermute | solution.py:326
  171.2 104.1 %reduce-scatter.4.cloned.1.call-start = ((), (), s32[]{:S(2)}) async-start(), calls=%async_computation.3 | async-start | bytes 1310720 | tf_op jit(solution)/shard_map/reduce_scatter | solution.py:496
  171.2 20.3 %collective-permute-start.19 = (bf16[4,64,256]{2,1,0:T(8,128)(2,1)S(1)}, bf16[4,64,256]{2,1,0:T(8,128)(2,1)S(1)}, u32[]{:S(2)}, u32[]{:S(2)}) collective-permute-start(bf16[4,64,256]{2,1,0:T(8,128)(2,1)S(1)} %fusion.17), channel_id=1, source_target_pairs={{0,4},{2,6},{4,0},{6,2},{8,12},{10,14},{12,8},{14,10},{16,20},{18,... | collective-permute-start | bytes 393224 | tf_op jit(solution)/shard_map/ppermute | solution.py:326
  171.7 23.3 %collective-permute-start.21 = (bf16[4,64,256]{2,1,0:T(8,128)(2,1)}, bf16[4,64,256]{2,1,0:T(8,128)(2,1)S(1)}, u32[]{:S(2)}, u32[]{:S(2)}) collective-permute-start(bf16[4,64,256]{2,1,0:T(8,128)(2,1)} %fusion.18), channel_id=1, source_target_pairs={{0,2},{2,0},{4,6},{6,4},{8,10},{10,8},{12,14},{14,12},{16,18},{18,... | collective-permute-start | bytes 393224 | tf_op jit(solution)/shard_map/ppermute | solution.py:326
  173.5 26.5 %collective-permute-start.25 = (bf16[4,192,256]{2,1,0:T(8,128)(2,1)S(1)}, bf16[4,192,256]{2,1,0:T(8,128)(2,1)S(1)}, u32[]{:S(2)}, u32[]{:S(2)}) collective-permute-start(bf16[4,192,256]{2,1,0:T(8,128)(2,1)S(1)} %fusion.11), channel_id=1, source_target_pairs={{0,4},{2,6},{4,0},{6,2},{8,12},{10,14},{12,8},{14,10},{16,20},{18,... | collective-permute-start | bytes 1179656 | tf_op jit(solution)/shard_map/ppermute | solution.py:326
  191.6 43.6 %collective-permute-start.30 = (bf16[4,2,384,256]{3,2,0,1:T(8,128)(2,1)S(1)}, bf16[4,2,384,256]{3,2,0,1:T(8,128)(2,1)}, u32[]{:S(2)}, u32[]{:S(2)}) collective-permute-start(bf16[4,2,384,256]{3,2,0,1:T(8,128)(2,1)S(1)} %copy.114), channel_id=1, source_target_pairs={{0,2},{2,0},{4,6},{6,4},{8,10},{10,8},{12,14},{14,12},{16,18},{18,... | collective-permute-start | bytes 4718600 | tf_op jit(solution)/shard_map/ppermute | solution.py:326
  194.4 37.5 %collective-permute-start.27 = (bf16[4,192,256]{2,1,0:T(8,128)(2,1)S(1)}, bf16[4,192,256]{2,1,0:T(8,128)(2,1)S(1)}, u32[]{:S(2)}, u32[]{:S(2)}) collective-permute-start(bf16[4,192,256]{2,1,0:T(8,128)(2,1)S(1)} %fusion.13), channel_id=1, source_target_pairs={{0,2},{2,0},{4,6},{6,4},{8,10},{10,8},{12,14},{14,12},{16,18},{18,... | collective-permute-start | bytes 1179656 | tf_op jit(solution)/shard_map/ppermute | solution.py:326
  195.0 46.9 %collective-permute-start.32 = (bf16[4,2,384,256]{3,2,0,1:T(8,128)(2,1)S(1)}, bf16[4,2,384,256]{3,2,0,1:T(8,128)(2,1)}, u32[]{:S(2)}, u32[]{:S(2)}) collective-permute-start(bf16[4,2,384,256]{3,2,0,1:T(8,128)(2,1)S(1)} %copy.117), channel_id=1, source_target_pairs={{0,4},{2,6},{4,0},{6,2},{8,12},{10,14},{12,8},{14,10},{16,20},{18,... | collective-permute-start | bytes 4718600 | tf_op jit(solution)/shard_map/ppermute | solution.py:326
  234.2 65.4 %reduce-scatter.6.cloned.1.call-start = ((), (), s32[]{:S(2)}) async-start(), calls=%async_computation.4 | async-start | bytes 1966080 | tf_op jit(solution)/shard_map/reduce_scatter | solution.py:496
  237.8 14.6 %collective-permute-start.31 = (bf16[4,384,256]{2,1,0:T(8,128)(2,1)}, bf16[4,384,256]{2,1,0:T(8,128)(2,1)}, u32[]{:S(2)}, u32[]{:S(2)}) collective-permute-start(bf16[4,384,256]{2,1,0:T(8,128)(2,1)} %fusion.3), channel_id=1, source_target_pairs={{0,4},{2,6},{4,0},{6,2},{8,12},{10,14},{12,8},{14,10},{16,20},{18,... | collective-permute-start | bytes 2359304 | tf_op jit(solution)/shard_map/ppermute | solution.py:326
  243.3 13.7 %collective-permute-start.33 = (bf16[4,384,256]{2,1,0:T(8,128)(2,1)S(1)}, bf16[4,384,256]{2,1,0:T(8,128)(2,1)}, u32[]{:S(2)}, u32[]{:S(2)}) collective-permute-start(bf16[4,384,256]{2,1,0:T(8,128)(2,1)S(1)} %fusion.4), channel_id=1, source_target_pairs={{0,2},{2,0},{4,6},{6,4},{8,10},{10,8},{12,14},{14,12},{16,18},{18,... | collective-permute-start | bytes 2359304 | tf_op jit(solution)/shard_map/ppermute | solution.py:326
  245.7 26.8 %collective-permute-start.9 = (f32[128,1024]{1,0:T(8,128)}, f32[128,1024]{1,0:T(8,128)S(1)}, u32[]{:S(2)}, u32[]{:S(2)}) collective-permute-start(f32[128,1024]{1,0:T(8,128)} %get-tuple-element.131), channel_id=1, source_target_pairs={{0,1},{1,0},{2,3},{3,2},{4,5},{5,4},{6,7},{7,6},{8,9},{9,8},{10,11... | collective-permute-start | bytes 1572872 | tf_op jit(solution)/shard_map/ppermute | solution.py:323
  245.9 14.8 %collective-permute-start.13 = (f32[4,912]{1,0:T(4,128)S(1)}, f32[4,912]{1,0:T(4,128)S(1)}, u32[]{:S(2)}, u32[]{:S(2)}) collective-permute-start(f32[4,912]{1,0:T(4,128)S(1)} %pad_maximum_fusion.6), channel_id=1, source_target_pairs={{0,8},{2,10},{4,12},{6,14},{8,0},{10,2},{12,4},{14,6},{16,24},{18,... | collective-permute-start | bytes 43784 | tf_op jit(solution)/shard_map/ppermute | solution.py:326
  (54 other events, 364.4 us)
Sparse Core Ops, SparseCore 0:
  171.3 23.5 reduce-scatter.7
  234.3 28.6 reduce-scatter.3
  265.5 34.0 reduce-scatter.5
